TPU v7x, 128 devices: a whole 4x4x4 slice. The times are simulated.
128 devices in a mesh: rows: 16 (over y, x), tensor: 8 (over z, core).
Axes of the slice: x: 4, y: 4, z: 4, core: 2. Of those that a mesh axis runs over, the one named last changes fastest.
Arguments:
- tokens: bfloat16 [16384, 4096], P('rows'), may hold values from -6 to 6
- grid_sizes: int32 [16, 4, 2], replicated, may hold values from 8 to 22, as said below
- owners: int32 [4096, 1], replicated, may hold values from 0 to 15; in each aligned block of 256 rows (0 to 255, 256 to 511, ...) at most 24 rows name the same one
- ln_gain: float32 [4096], replicated, may hold values from 0.5 to 1.5
- ln_bias: float32 [4096], replicated, may hold values from -4 to 4
- w_qkv: bfloat16 [4096, 3, 4096], P('rows', None, 'tensor')
- w_out: bfloat16 [4096, 4096], P('tensor', 'rows'), may hold values from -0.09375 to 0.09375
- layer_scale: float32 [4096], replicated, may hold values from 0.2 to 2
- merge_gain: float32 [4, 4096], replicated, may hold values from 0.5 to 1.5
- merge_bias: float32 [4, 4096], replicated, may hold values from -4 to 4
- w_merge: bfloat16 [4, 4096, 2048], P(None, 'rows', 'tensor'), may hold values from -0.046875 to 0.046875
Outputs:
- received: bfloat16 [6144, 2048], P('rows', 'tensor')
Inputs may be any that keep to these rules, and one draw needn't show every extreme that they name: `grid_sizes`: image grids have even sides with 96 to 396 patches, so images hold 101 to 401 tokens; each block's images together hold at most 1024 tokens; in every draw some image has 22 x 18 patches (height 22, width 18) and some has 8 x 12 (height 8, width 12). `owners`: no owner is named by more than 24 of the 256 merged slots of one block.
All inputs are finite; a program needn't handle non-finite values.
Results may differ from a plain program's by a relative error of at most 0.013.
Values may be sent and summed in bfloat16 or wider, within the bound.
A program may use at most 128 MiB of HBM per device.

v0:
```python
import functools
import math

import jax
import jax.numpy as jnp
from jax import lax
from jax.experimental import pallas as pl
from jax.experimental.pallas import tpu as pltpu
from jax.sharding import PartitionSpec as P

MESH = pl.DeviceIdType.MESH
F32 = jnp.float32
BF16 = jnp.bfloat16
HEAD_DIM = 128
PREFIX = 5


class Gather:
    def __init__(self, src, region, send, recv, place):
        self.src, self.region, self.send, self.recv_sem = src, region, send, recv
        self.y, self.x, self.t = place
        table = [
            ((0, 0), None, (1, 0)),
            ((0, 0), None, (-1, 0)),
            ((0, 0), None, (0, 1)),
            ((0, 0), None, (0, -1)),
            ((-1, 0), 0, (1, 0)),
            ((1, 0), 1, (-1, 0)),
            ((-1, 0), None, (0, 1)),
            ((-1, 0), None, (0, -1)),
            ((1, 0), None, (0, 1)),
            ((1, 0), None, (0, -1)),
            ((2, 0), None, (0, 1)),
            ((2, 0), None, (0, -1)),
        ]
        for first in (0, -1, 1, 2):
            table.append(((first, -1), 0, (0, 1)))
            table.append(((first, 1), 1, (0, -1)))
        self.table = table

    def slot(self, half, first, second):
        dx, dy = (first, second) if half == 0 else (second, first)
        return lax.rem(self.y + (dy % 4), 4) * 4 + lax.rem(self.x + (dx % 4), 4)

    def copy(self, half, i):
        (first, second), part, to = self.table[i]
        slot = self.slot(half, first, second)
        dst = self.region(half, slot, part)
        src = self.src(half) if self.src is not None and i < 4 else dst
        return pltpu.make_async_remote_copy(
            src_ref=src,
            dst_ref=dst,
            send_sem=self.send.at[half, i],
            recv_sem=self.recv_sem.at[half, i],
            device_id=(self.slot(half, *to), self.t),
            device_id_type=MESH,
        )

    def start(self, *which):
        for i in which:
            for half in (0, 1):
                self.copy(half, i).start()

    def recv(self, *which):
        for i in which:
            for half in (0, 1):
                self.copy(half, i).wait_recv()

    def r1(self):
        self.start(0, 1, 2, 3)

    def r2(self):
        self.recv(0, 1)
        self.start(4, 5, 6, 7, 8, 9)

    def r3(self):
        self.recv(4, 5)
        self.start(10, 11)

    def r4a(self):
        self.recv(2, 3)
        self.start(12, 13)

    def r4b(self):
        self.recv(6, 7, 8, 9)
        self.start(14, 15, 16, 17)

    def r4c(self):
        self.recv(10, 11)
        self.start(18, 19)

    def finish(self):
        self.recv(12, 13, 14, 15, 16, 17, 18, 19)

    def drain(self):
        for i in range(20):
            for half in (0, 1):
                self.copy(half, i).wait_send()


def dot(a, b):
    return jnp.dot(a, b, preferred_element_type=F32)


def kernel(
    tokens,
    wq,
    wo,
    wm,
    ln_gain,
    ln_bias,
    scale,
    merge_gain,
    merge_bias,
    grid_ref,
    own_ref,
    out,
    bufq,
    bufo,
    bufm,
    normed,
    acc,
    qb,
    kb,
    vb,
    att,
    tok,
    tokp,
    cos_ref,
    sin_ref,
    src_ref,
    segq_ref,
    pos_ref,
    wo_in,
    scale_own,
    gain_own,
    bias_own,
    fromsib,
    oppa,
    oppb,
    zprev,
    znext,
    stats,
    mpart,
    msib,
    mopp,
    mz,
    obuf,
    sq,
    rq,
    so,
    ro,
    sm,
    rm,
    local,
    sperm,
    rperm,
    ssib,
    rsib,
    sopp,
    ropp,
    sz,
    rz,
    sstat,
    rstat,
    smsib,
    rmsib,
    smopp,
    rmopp,
    smz,
    rmz,
    sout,
    rout,
):
    r = lax.axis_index("rows")
    t = lax.axis_index("tensor")
    y, x = lax.div(r, 4), lax.rem(r, 4)
    z, c = lax.div(t, 2), lax.rem(t, 2)
    place = (y, x, t)
    tiles = 4
    rows_tile = 256

    def zdev(offset, core=None):
        return lax.rem(z + offset % 4, 4) * 2 + (c if core is None else core)

    sibling = z * 2 + (1 - c)
    barrier = pltpu.get_barrier_semaphore()
    for step in range(1, 16):
        pl.semaphore_signal(
            barrier, inc=1, device_id=(lax.rem(r + step, 16), t), device_id_type=MESH
        )
    for step in range(1, 8):
        pl.semaphore_signal(
            barrier, inc=1, device_id=(r, lax.rem(t + step, 8)), device_id_type=MESH
        )
    pl.semaphore_wait(barrier, 22)

    def src_q(half):
        return wq.at[:, :, pl.ds(256 * half, 256)]

    def region_q(half, slot, part):
        if part is None:
            return bufq.at[half, slot]
        return bufq.at[half, slot, :, pl.ds(128 * part, 128)]

    def region_o(half, slot, part):
        if part is None:
            return bufo.at[pl.ds(4 * half, 4), slot]
        return bufo.at[pl.ds(4 * half + 2 * part, 2), slot]

    def region_m(half, slot, part):
        return bufm.at[half, slot] if part is None else bufm.at[half, slot, part]

    gq = Gather(src_q, region_q, sq, rq, place)
    go = Gather(None, region_o, so, ro, place)
    gm = Gather(None, region_m, sm, rm, place)

    gq.r1()

    def deal_piece(to):
        return wm.at[:, :, pl.ds(pl.multiple_of(to * 32, 32), 32), :]

    def deal_place(come):
        return bufm.at[:, r, :, :, pl.ds(pl.multiple_of(come * 256, 256), 256)]

    def deal_copy(step):
        to = lax.rem(t + step, 8)
        return pltpu.make_async_remote_copy(
            src_ref=deal_piece(to),
            dst_ref=deal_place(t),
            send_sem=sperm.at[step],
            recv_sem=rperm.at[step],
            device_id=(r, to),
            device_id_type=MESH,
        )

    def deal_wait(step):
        come = lax.rem(t + 8 - step, 8)
        pltpu.make_async_remote_copy(
            src_ref=deal_piece(come),
            dst_ref=deal_place(come),
            send_sem=sperm.at[step],
            recv_sem=rperm.at[step],
            device_id=(r, come),
            device_id_type=MESH,
        ).wait_recv()

    own_deal = pltpu.make_async_copy(deal_piece(t), deal_place(t), local.at[6])

    chunk = 256

    def tok_copy(i):
        rows = pl.ds(i * chunk, chunk)
        return pltpu.make_async_copy(tokens.at[rows], normed.at[rows], local.at[i])

    for i in range(4):
        tok_copy(i).start()
    own_q = [pltpu.make_async_copy(src_q(h), bufq.at[h, r], local.at[4 + h]) for h in (0, 1)]
    own_wo = pltpu.make_async_copy(wo, wo_in, local.at[7])
    for copy in own_q + [own_wo, own_deal]:
        copy.start()
    for step in range(1, 8):
        deal_copy(step).start()

    feature_tile = lax.div(t, 4) * 128

    def own_features(load):
        tiles_out = []
        for j in range(4):
            taken = None
            for q in range(4):
                v = load(pl.ds(pl.multiple_of(256 * (4 * j + q) + feature_tile, 128), 128))
                v = pltpu.roll(v, lax.rem(32 * q + 128 - 32 * lax.rem(t, 4), 128), 1)
                if q:
                    at = lax.broadcasted_iota(jnp.int32, v.shape, 1)
                    v = jnp.where(at >= 32 * q, v, taken)
                taken = v
            tiles_out.append(taken)
        return jnp.concatenate(tiles_out, axis=1)

    def norm_chunk(i):
        tok_copy(i).wait()
        step = 16

        def body(j, carry):
            at = pl.ds(pl.multiple_of(i * chunk + j * step, step), step)
            tok[at, :] = own_features(lambda cols: normed[at, cols].astype(F32)).astype(BF16)
            v = normed[at, :].astype(F32)
            mean = jnp.mean(v, axis=-1, keepdims=True)
            v = v - mean
            var = jnp.mean(v * v, axis=-1, keepdims=True)
            v = v * lax.rsqrt(var + 1e-6) * ln_gain[...] + ln_bias[...]
            normed[at, :] = v.astype(BF16)
            return carry

        lax.fori_loop(0, chunk // step, body, 0)

    grid = grid_ref[...]
    heights = [grid[:, 2 * i : 2 * i + 1] for i in range(4)]
    widths = [grid[:, 2 * i + 1 : 2 * i + 2] for i in range(4)]
    starts, merged_starts = [jnp.zeros((1, 1), jnp.int32)], [jnp.zeros((1, 1), jnp.int32)]
    for h, w in zip(heights, widths):
        starts.append(starts[-1] + PREFIX + h * w)
        merged_starts.append(merged_starts[-1] + ((h * w).astype(F32) * 0.25).astype(jnp.int32))
    lane = lax.broadcasted_iota(jnp.int32, (rows_tile, HEAD_DIM), 1)
    low = lax.rem(lane, 64) < 32

    freqs = jnp.exp2(lax.rem(lane[0:1, :], 32).astype(F32) * (-math.log2(100.0) / 32))

    def choose(at, edges, values):
        chosen = jnp.zeros(at.shape, jnp.int32) + values[0]
        for edge, value in zip(edges[1:4], values[1:4]):
            chosen = jnp.where(at >= edge, value, chosen)
        return chosen

    def tables(i, carry):
        at = pl.ds(pl.multiple_of(i * rows_tile, rows_tile), rows_tile)
        pos = lax.broadcasted_iota(jnp.int32, (rows_tile, HEAD_DIM), 0) + i * rows_tile
        local_pos = pos - choose(pos, starts, starts) - PREFIX
        patch = (local_pos >= 0) & (pos < starts[4])
        flat = jnp.where(patch, local_pos, 0).astype(F32)
        width = choose(pos, starts, widths).astype(F32)
        row = jnp.floor((flat + 0.5) / width)
        angle = jnp.where(lane < 64, row, flat - row * width) * freqs
        cos_ref[at, :] = jnp.cos(angle)
        sine = jnp.sin(angle)
        sin_ref[at, :] = jnp.where(low, -sine, sine)
        return carry

    def slots_layout():
        m = lax.broadcasted_iota(jnp.int32, (rows_tile, HEAD_DIM), 0)
        live = m < merged_starts[4]
        width = choose(m, merged_starts, widths).astype(F32)
        first = choose(m, merged_starts, starts).astype(F32) + PREFIX
        offset = (m - choose(m, merged_starts, merged_starts)).astype(F32)
        row = jnp.floor((offset + 0.5) / (0.5 * width))
        corner = first + (2.0 * row) * width + 2.0 * (offset - row * (0.5 * width))
        for k in range(4):
            source = corner + width * float(k // 2) + float(k % 2)
            src_ref[k * rows_tile : (k + 1) * rows_tile, :] = jnp.where(live, source, 0.0).astype(
                jnp.int32
            )
        segq_ref[...] = jnp.where(live, choose(m, merged_starts, [0, 1, 2, 3]), 0)

        own_row = own_ref[...]
        own_col = jnp.broadcast_to(own_row.astype(F32), (HEAD_DIM, 256)).T[:, 0:1]
        before = lax.broadcasted_iota(jnp.int32, (256, 256), 0) < lax.broadcasted_iota(
            jnp.int32, (256, 256), 1
        )
        hit = before & (own_col == own_row.astype(F32))
        rank = jnp.sum(jnp.where(hit, 1.0, 0.0), axis=0, keepdims=True).astype(jnp.int32)
        live_row = lax.broadcasted_iota(jnp.int32, (1, 256), 1) < merged_starts[4]
        pos_ref[...] = jnp.where(live_row, own_row * 32 + rank, -1)

    key_pos = lax.broadcasted_iota(jnp.int32, (1, 1024), 1)
    segk = jnp.zeros((1, 1024), jnp.int32)
    for edge in starts[1:]:
        segk = segk + (key_pos >= edge).astype(jnp.int32)

    def project(slots, first=False):
        for half in (0, 1):
            where = [gq.slot(half, *s) for s in slots]

            def body(i, carry, half=half, where=where):
                out_cols = pl.ds(pl.multiple_of(i * 256, 256), 256)
                total = None
                for w in where:
                    cols = pl.ds(pl.multiple_of(w * 256, 256), 256)
                    term = dot(normed[:, cols], bufq[half, w, i])
                    total = term if total is None else total + term
                if first:
                    acc[half, :, out_cols] = total
                else:
                    acc[half, :, out_cols] += total
                return carry

            lax.fori_loop(0, 3, body, 0)

    for i in range(3):
        norm_chunk(i)
    for copy in own_q:
        copy.wait()
    gq.r2()
    norm_chunk(3)
    gq.r4a()
    project([(0, 0), (-1, 0), (1, 0)], first=True)
    project([(0, -1), (0, 1)])
    gq.r3()
    project([(2, 0)])
    lax.fori_loop(0, tiles, tables, 0)
    slots_layout()
    own_wo.wait()
    turned = wo_in[...].astype(F32).T.astype(BF16)
    for i in range(8):
        bufo[i, r] = turned[32 * i : 32 * i + 32, :]
    scale_own[...] = own_features(lambda cols: scale[:, cols])
    gain_own[...] = own_features(lambda cols: merge_gain[:, cols])
    bias_own[...] = own_features(lambda cols: merge_bias[:, cols])
    gq.r4b()
    go.r1()
    project([(-1, -1), (-1, 1), (1, -1), (1, 1)])
    gq.r4c()
    project([(2, -1), (2, 1)])
    gq.recv(12, 13, 14, 15)
    project([(0, 2), (-1, 2)])
    go.r2()
    go.r4a()
    gq.recv(16, 17, 18, 19)
    project([(1, 2), (2, 2)])
    go.r3()

    def rotate(i, carry):
        at = pl.ds(pl.multiple_of(i * rows_tile, rows_tile), rows_tile)
        cosine, sine = cos_ref[at, :], sin_ref[at, :]
        for head in range(4):
            half, inner = divmod(head, 2)
            for dst, base in ((qb, 0), (kb, 256)):
                v = acc[half, at, base + inner * 128 : base + inner * 128 + 128]
                partner = jnp.where(low, pltpu.roll(v, 96, 1), pltpu.roll(v, 32, 1))
                dst[at, head * 128 : head * 128 + 128] = (v * cosine + partner * sine).astype(BF16)
            vb[at, head * 128 : head * 128 + 128] = acc[
                half, at, 512 + inner * 128 : 512 + inner * 128 + 128
            ].astype(BF16)
        return carry

    lax.fori_loop(0, tiles, rotate, 0)

    factor = HEAD_DIM ** (-0.5) / math.log(2.0)

    def attend(k):
        at = slice(k * rows_tile, (k + 1) * rows_tile)
        pick = (
            lax.broadcasted_iota(jnp.int32, (rows_tile, 1024), 1) == src_ref[at, 0:1]
        ).astype(BF16)
        att[at, :] = dot(pick, qb[...]).astype(BF16)
        tokp[at, :] = dot(pick, tok[...]).astype(BF16)

        def body(head, carry):
            cols = pl.ds(pl.multiple_of(head * 128, 128), 128)
            s = lax.dot_general(
                att[at, cols], kb[:, cols], (((1,), (1,)), ((), ())), preferred_element_type=F32
            )
            s = jnp.where(segq_ref[:, 0:1] == segk, s, -jnp.inf)
            top = jnp.max(s, axis=-1, keepdims=True)
            e = jnp.exp2((s - top) * factor)
            total = jnp.sum(e, axis=-1, keepdims=True)
            o = dot(e.astype(BF16), vb[:, cols])
            att[at, cols] = (o / total).astype(BF16)
            return carry

        lax.fori_loop(0, 4, body, 0)

    def out_project(to):
        def body(j, carry):
            weight = bufo[to, pl.ds(j * 8, 8)].reshape(256, 512)
            total = lax.dot_general(
                att[...], weight, (((1,), (1,)), ((), ())), preferred_element_type=F32
            )
            cols = pl.ds(pl.multiple_of(to * 512 + j * 256, 256), 256)
            normed[:, cols] = total.astype(BF16)
            return carry

        lax.fori_loop(0, 2, body, 0)

    def chunk_of(tensor, lo=0, rows=1024):
        return normed.at[pl.ds(lo, rows), pl.ds(pl.multiple_of(tensor * 512, 512), 512)]

    def sib_copy(dz):
        return pltpu.make_async_remote_copy(
            src_ref=chunk_of(zdev(dz, 1 - c)),
            dst_ref=fromsib.at[dz % 4],
            send_sem=ssib.at[dz % 4],
            recv_sem=rsib.at[dz % 4],
            device_id=(r, sibling),
            device_id_type=MESH,
        )

    def opp_copy(which):
        return pltpu.make_async_remote_copy(
            src_ref=chunk_of(zdev(2), 512 * which, 512),
            dst_ref=(oppa, oppb)[which],
            send_sem=sopp.at[which],
            recv_sem=ropp.at[which],
            device_id=(r, zdev(1 if which == 0 else -1)),
            device_id_type=MESH,
        )

    def z_copy(which, part):
        to = zdev(1 if which == 0 else -1)
        return pltpu.make_async_remote_copy(
            src_ref=chunk_of(to, 512 * part, 512),
            dst_ref=(zprev, znext)[which].at[pl.ds(512 * part, 512)],
            send_sem=sz.at[which, part],
            recv_sem=rz.at[which, part],
            device_id=(r, to),
            device_id_type=MESH,
        )

    def to_sibling(dz):
        out_project(zdev(dz, 1 - c))
        sib_copy(dz).start()

    def to_own(dz):
        out_project(zdev(dz))

    def partial(dz):
        out_project(zdev(dz, 1 - c))
        sib_copy(dz).start()
        out_project(zdev(dz))

    def add_sibling(dz):
        sib_copy(dz).wait_recv()

        def body(i, carry):
            ref = chunk_of(zdev(dz), pl.multiple_of(i * 256, 256), 256)
            other = fromsib[dz % 4, pl.ds(pl.multiple_of(i * 256, 256), 256), :]
            ref[...] = (ref[...].astype(F32) + other.astype(F32)).astype(BF16)
            return carry

        lax.fori_loop(0, 4, body, 0)

    def pass_on(which):
        opp_copy(which).wait_recv()
        for i in (0, 1):
            ref = chunk_of(zdev(1 if which == 0 else -1), 512 * which + 256 * i, 256)
            other = (oppa, oppb)[which][256 * i : 256 * i + 256, :]
            ref[...] = (ref[...].astype(F32) + other.astype(F32)).astype(BF16)
        z_copy(which, which).start()

    sums = []

    def finish_rows(k):
        at = slice(k * rows_tile, (k + 1) * rows_tile)
        total = (
            chunk_of(t, k * rows_tile, rows_tile)[...].astype(F32)
            + fromsib[0, at, :].astype(F32)
            + zprev[at, :].astype(F32)
            + znext[at, :].astype(F32)
        )
        res = tokp[at, :].astype(F32) + scale_own[...] * total
        acc[0, at, 0:512] = res
        sums.append(jnp.sum(res, axis=-1, keepdims=True))

    go.r4b()
    attend(0)
    go.r4c()
    own_deal.wait()
    for step in range(1, 8):
        deal_wait(step)
    gm.r1()
    attend(1)
    attend(2)
    attend(3)
    go.finish()
    to_sibling(2)
    to_own(2)
    to_sibling(1)
    add_sibling(2)
    opp_copy(0).start()
    opp_copy(1).start()
    gm.r2()
    to_own(1)
    to_sibling(-1)
    add_sibling(1)
    z_copy(0, 1).start()
    gm.r4a()
    to_own(-1)
    to_sibling(0)
    add_sibling(-1)
    z_copy(1, 0).start()
    gm.r3()
    pass_on(0)
    pass_on(1)
    to_own(0)
    gm.r4b()
    gm.r4c()
    sib_copy(0).wait_recv()
    z_copy(0, 1).wait_recv()
    z_copy(1, 1).wait_recv()
    z_copy(0, 0).wait_recv()
    z_copy(1, 0).wait_recv()
    for k in range(4):
        finish_rows(k)

    mean_l = (sums[0] + sums[1] + sums[2] + sums[3]) * (1.0 / 2048)
    m2 = None
    for k in range(4):
        d = acc[0, k * 256 : (k + 1) * 256, 0:512] - mean_l
        term = jnp.sum(d * d, axis=-1, keepdims=True)
        m2 = term if m2 is None else m2 + term
    packed = jnp.where(lane == 0, mean_l, m2)
    stats[0] = packed.T[0:8, :]

    def stat_copy(step):
        return pltpu.make_async_remote_copy(
            src_ref=stats.at[0],
            dst_ref=stats.at[step],
            send_sem=sstat.at[step],
            recv_sem=rstat.at[step],
            device_id=(r, lax.rem(t + step, 8)),
            device_id_type=MESH,
        )

    for step in range(1, 8):
        stat_copy(step).start()
    gm.finish()
    for step in range(1, 8):
        stat_copy(step).wait_recv()
    means = [stats[i][0:1, :] for i in range(8)]
    m2s = [stats[i][1:2, :] for i in range(8)]
    mean = functools.reduce(lambda a, b: a + b, means) * 0.125
    total2 = functools.reduce(lambda a, b: a + b, m2s)
    for m in means:
        total2 = total2 + 2048.0 * (m - mean) * (m - mean)
    rs = lax.rsqrt(total2 * (1.0 / 16384) + 1e-6)
    row = lax.broadcasted_iota(jnp.int32, (128, 256), 0)
    back = jnp.where(row == 0, mean, rs).T
    mean_c, rs_c = back[:, 0:1], back[:, 1:2]
    for k in range(4):
        at = slice(k * rows_tile, (k + 1) * rows_tile)
        v = (acc[0, at, 0:512] - mean_c) * rs_c
        v = v * gain_own[k : k + 1, :] + bias_own[k : k + 1, :]
        att[at, :] = v.astype(BF16)

    def merge_chunk(core, dz):
        to = zdev(dz, core)
        cols = pl.ds(pl.multiple_of(to * 256, 256), 256)
        total = None
        for k in range(4):
            for j in (0, 1):
                term = dot(
                    att[k * 256 : (k + 1) * 256, j * 256 : j * 256 + 256],
                    bufm[k // 2, 8 * j : 8 * j + 8, k % 2, :, cols].reshape(256, 256),
                )
                total = term if total is None else total + term
        return total

    def msib_copy(dz):
        return pltpu.make_async_remote_copy(
            src_ref=mpart.at[1 - c, dz % 4],
            dst_ref=msib.at[dz % 4],
            send_sem=smsib.at[dz % 4],
            recv_sem=rmsib.at[dz % 4],
            device_id=(r, sibling),
            device_id_type=MESH,
        )

    def mopp_copy(which):
        return pltpu.make_async_remote_copy(
            src_ref=mpart.at[c, 2, pl.ds(128 * which, 128)],
            dst_ref=mopp.at[which],
            send_sem=smopp.at[which],
            recv_sem=rmopp.at[which],
            device_id=(r, zdev(1 if which == 0 else -1)),
            device_id_type=MESH,
        )

    def mz_copy(which, part):
        return pltpu.make_async_remote_copy(
            src_ref=mpart.at[c, 1 if which == 0 else 3, pl.ds(128 * part, 128)],
            dst_ref=mz.at[which, pl.ds(128 * part, 128)],
            send_sem=smz.at[which, part],
            recv_sem=rmz.at[which, part],
            device_id=(r, zdev(1 if which == 0 else -1)),
            device_id_type=MESH,
        )

    def merge_own(dz):
        total = merge_chunk(c, dz)
        msib_copy(dz).wait_recv()
        return total + msib[dz % 4].astype(F32)

    for dz in (2, 1, -1, 0):
        mpart[1 - c, dz % 4] = merge_chunk(1 - c, dz).astype(BF16)
        msib_copy(dz).start()
    mpart[c, 2] = merge_own(2).astype(BF16)
    for which in (0, 1):
        mopp_copy(which).start()
    mpart[c, 1] = merge_own(1).astype(BF16)
    mz_copy(0, 1).start()
    mpart[c, 3] = merge_own(-1).astype(BF16)
    mz_copy(1, 0).start()
    for which, index in ((0, 1), (1, 3)):
        mopp_copy(which).wait_recv()
        rows = pl.ds(128 * which, 128)
        mpart[c, index, rows, :] = (
            mpart[c, index, rows, :].astype(F32) + mopp[which].astype(F32)
        ).astype(BF16)
        mz_copy(which, which).start()
    merged = merge_own(0)
    for which in (0, 1):
        for part in (0, 1):
            mz_copy(which, part).wait_recv()
    merged = (merged + mz[0].astype(F32) + mz[1].astype(F32)).astype(BF16)

    place_row = (lax.broadcasted_iota(jnp.int32, (512, 256), 0) == pos_ref[...]).astype(BF16)
    obuf[...] = dot(place_row, merged).astype(BF16).reshape(16, 32, 256)

    def out_copy(step):
        to = lax.rem(r + step, 16)
        return pltpu.make_async_remote_copy(
            src_ref=obuf.at[to],
            dst_ref=out.at[r],
            send_sem=sout.at[step],
            recv_sem=rout.at[step],
            device_id=(to, t),
            device_id_type=MESH,
        )

    def out_wait(step):
        come = lax.rem(r + 16 - step, 16)
        pltpu.make_async_remote_copy(
            src_ref=obuf.at[come],
            dst_ref=out.at[come],
            send_sem=sout.at[step],
            recv_sem=rout.at[step],
            device_id=(come, t),
            device_id_type=MESH,
        ).wait_recv()

    own_out = pltpu.make_async_copy(obuf.at[r], out.at[r], local.at[9])
    for step in range(1, 16):
        out_copy(step).start()
    own_out.start()

    for step in range(1, 8):
        deal_copy(step).wait_send()
    for g in (gq, go, gm):
        g.drain()
    for dz in range(4):
        sib_copy(dz).wait_send()
    for which in (0, 1):
        opp_copy(which).wait_send()
        for part in (0, 1):
            z_copy(which, part).wait_send()
    for step in range(1, 8):
        stat_copy(step).wait_send()
    for dz in range(4):
        msib_copy(dz).wait_send()
    for which in (0, 1):
        mopp_copy(which).wait_send()
        for part in (0, 1):
            mz_copy(which, part).wait_send()
    own_out.wait()
    for step in range(1, 16):
        out_wait(step)
        out_copy(step).wait_send()


def per_device(
    tokens,
    grid_sizes,
    owners,
    ln_gain,
    ln_bias,
    w_qkv,
    w_out,
    layer_scale,
    merge_gain,
    merge_bias,
    w_merge,
):
    own_row = lax.dynamic_slice_in_dim(owners, lax.axis_index("rows") * 256, 256).reshape(1, 256)
    grid_row = lax.dynamic_slice_in_dim(grid_sizes, lax.axis_index("rows"), 1).reshape(1, 8)
    wq = w_qkv.transpose(1, 0, 2)
    wm = w_merge.reshape(2, 2, 256, 256)

    any_space = pl.BlockSpec(memory_space=pl.ANY)
    vmem = pl.BlockSpec(memory_space=pltpu.VMEM)
    dma = pltpu.SemaphoreType.DMA
    out = pl.pallas_call(
        kernel,
        out_shape=jax.ShapeDtypeStruct((16, 32, 256), BF16),
        in_specs=[any_space] * 4 + [vmem] * 7,
        out_specs=any_space,
        scratch_shapes=[
            pltpu.VMEM((2, 16, 3, 256, 256), BF16),
            pltpu.VMEM((8, 16, 32, 512), BF16),
            pltpu.VMEM((2, 16, 2, 32, 2048), BF16),
            pltpu.VMEM((1024, 4096), BF16),
            pltpu.VMEM((2, 1024, 768), F32),
            pltpu.VMEM((1024, 512), BF16),
            pltpu.VMEM((1024, 512), BF16),
            pltpu.VMEM((1024, 512), BF16),
            pltpu.VMEM((1024, 512), BF16),
            pltpu.VMEM((1024, 512), BF16),
            pltpu.VMEM((1024, 512), BF16),
            pltpu.VMEM((1024, 128), F32),
            pltpu.VMEM((1024, 128), F32),
            pltpu.VMEM((1024, 128), jnp.int32),
            pltpu.VMEM((256, 128), jnp.int32),
            pltpu.VMEM((1, 256), jnp.int32),
            pltpu.VMEM((512, 256), BF16),
            pltpu.VMEM((1, 512), F32),
            pltpu.VMEM((4, 512), F32),
            pltpu.VMEM((4, 512), F32),
            pltpu.VMEM((4, 1024, 512), BF16),
            pltpu.VMEM((512, 512), BF16),
            pltpu.VMEM((512, 512), BF16),
            pltpu.VMEM((1024, 512), BF16),
            pltpu.VMEM((1024, 512), BF16),
            pltpu.VMEM((8, 8, 256), F32),
            pltpu.VMEM((2, 4, 256, 256), BF16),
            pltpu.VMEM((4, 256, 256), BF16),
            pltpu.VMEM((2, 128, 256), BF16),
            pltpu.VMEM((2, 256, 256), BF16),
            pltpu.VMEM((16, 32, 256), BF16),
            dma((2, 20)),
            dma((2, 20)),
            dma((2, 20)),
            dma((2, 20)),
            dma((2, 20)),
            dma((2, 20)),
            dma((10,)),
            dma((8,)),
            dma((8,)),
            dma((4,)),
            dma((4,)),
            dma((2,)),
            dma((2,)),
            dma((2, 2)),
            dma((2, 2)),
            dma((8,)),
            dma((8,)),
            dma((4,)),
            dma((4,)),
            dma((2,)),
            dma((2,)),
            dma((2, 2)),
            dma((2, 2)),
            dma((16,)),
            dma((16,)),
        ],
        compiler_params=pltpu.CompilerParams(
            collective_id=0, has_side_effects=True, vmem_limit_bytes=63 * 2**20
        ),
    )(
        tokens,
        wq,
        w_out,
        wm,
        ln_gain[None],
        ln_bias[None],
        layer_scale[None],
        merge_gain,
        merge_bias,
        grid_row,
        own_row,
    )
    return out[:, :24].reshape(384, 256)


def solution(mesh):
    return jax.shard_map(
        per_device,
        mesh=mesh,
        in_specs=(
            P("rows", None),
            P(),
            P(),
            P(),
            P(),
            P("rows", None, "tensor"),
            P("tensor", "rows"),
            P(),
            P(),
            P(),
            P(None, "rows", "tensor"),
        ),
        out_specs=P("rows", "tensor"),
        check_vma=False,
    )
```

profile of v0, /device:TPU:0, one launch (start us, length us, event | category | flops | bytes accessed | tf_op | source)
XLA Modules:
  0.0 171.8 jit_solution(3413189004589805334)
XLA Ops:
  0.0 0.0 copy-start
  0.0 0.7 copy-done
  0.7 0.6 dynamic-slice_bitcast_fusion.own_ref
  1.3 0.9 dynamic-slice_reduce_fusion
  2.2 0.7 reshape.13.grid_ref
  2.8 167.3 %shard_map.109 = bf16[16,32,256]{2,1,0:T(8,128)(2,1)} custom-call(bf16[1024,4096]{1,0:T(8,128)(2,1)} %tokens.1, bf16[3,256,512]{2,1,0:T(8,128)(2,1)} %bitcast.8, bf16[512,256]{1,0:T(8,128)(2,1)} %wo.1, bf16[2,2,256,256]{3,2,1,0:T(8,128)(2,1)} %bitcast.9, f32[1,4096]{1,0:T(1,128)} %bitcast.10, f32[1,4096]{1,0:T(1,128)} %bitcast.11, f32[1,4096]{1,0:T(1,128)} %bitcast.12, ...), custom_call_target="tpu_custom_call" | custom-call | tf_op jit(solution)/shard_map/pallas_call | solution.py:771
  170.2 1.6 slice.3
Async XLA Ops:
  0.0 0.7 copy-start
where the time goes:
time: 172 us
  Pallas kernels  167 us (97%)
  local copies, waits for them, and re-layouts  4.47 us (3%)
    pallas_call x1, Pallas kernels, per_device(): pl.pallas_call(kernel, out_shape=jax.ShapeDtypeStruct((16, 32, 256), BF16...  167 us

commit v1 on v0

--- a/solution.py
+++ b/solution.py
@@ -450,14 +450,14 @@
 
         lax.fori_loop(0, 4, body, 0)
 
-    def out_project(to):
+    def out_project(to, lo=0, rows=1024):
         def body(j, carry):
             weight = bufo[to, pl.ds(j * 8, 8)].reshape(256, 512)
             total = lax.dot_general(
-                att[...], weight, (((1,), (1,)), ((), ())), preferred_element_type=F32
+                att[lo : lo + rows, :], weight, (((1,), (1,)), ((), ())), preferred_element_type=F32
             )
             cols = pl.ds(pl.multiple_of(to * 512 + j * 256, 256), 256)
-            normed[:, cols] = total.astype(BF16)
+            normed[lo : lo + rows, cols] = total.astype(BF16)
             return carry
 
         lax.fori_loop(0, 2, body, 0)
@@ -475,6 +475,16 @@
             device_id_type=MESH,
         )
 
+    def sib_half(part):
+        return pltpu.make_async_remote_copy(
+            src_ref=chunk_of(zdev(2, 1 - c), 512 * part, 512),
+            dst_ref=fromsib.at[2, pl.ds(512 * part, 512)],
+            send_sem=ssib.at[2 + 2 * part],
+            recv_sem=rsib.at[2 + 2 * part],
+            device_id=(r, sibling),
+            device_id_type=MESH,
+        )
+
     def opp_copy(which):
         return pltpu.make_async_remote_copy(
             src_ref=chunk_of(zdev(2), 512 * which, 512),
@@ -501,11 +511,6 @@
         sib_copy(dz).start()
 
     def to_own(dz):
-        out_project(zdev(dz))
-
-    def partial(dz):
-        out_project(zdev(dz, 1 - c))
-        sib_copy(dz).start()
         out_project(zdev(dz))
 
     def add_sibling(dz):
@@ -529,15 +534,19 @@
 
     sums = []
 
-    def finish_rows(k):
+    def begin_rows(k):
         at = slice(k * rows_tile, (k + 1) * rows_tile)
         total = (
             chunk_of(t, k * rows_tile, rows_tile)[...].astype(F32)
             + fromsib[0, at, :].astype(F32)
-            + zprev[at, :].astype(F32)
-            + znext[at, :].astype(F32)
-        )
-        res = tokp[at, :].astype(F32) + scale_own[...] * total
+            + (znext if k < 2 else zprev)[at, :].astype(F32)
+        )
+        acc[0, at, 0:512] = tokp[at, :].astype(F32) + scale_own[...] * total
+
+    def finish_rows(k):
+        at = slice(k * rows_tile, (k + 1) * rows_tile)
+        late = (zprev if k < 2 else znext)[at, :].astype(F32)
+        res = acc[0, at, 0:512] + scale_own[...] * late
         acc[0, at, 0:512] = res
         sums.append(jnp.sum(res, axis=-1, keepdims=True))
 
@@ -552,12 +561,19 @@
     attend(2)
     attend(3)
     go.finish()
-    to_sibling(2)
-    to_own(2)
+    for part in (0, 1):
+        out_project(zdev(2, 1 - c), 512 * part, 512)
+        sib_half(part).start()
+    for part in (0, 1):
+        out_project(zdev(2), 512 * part, 512)
+        sib_half(part).wait_recv()
+        for i in (0, 1):
+            lo = 512 * part + 256 * i
+            ref = chunk_of(zdev(2), lo, 256)
+            other = fromsib[2, lo : lo + 256, :]
+            ref[...] = (ref[...].astype(F32) + other.astype(F32)).astype(BF16)
+        opp_copy(part).start()
     to_sibling(1)
-    add_sibling(2)
-    opp_copy(0).start()
-    opp_copy(1).start()
     gm.r2()
     to_own(1)
     to_sibling(-1)
@@ -574,11 +590,15 @@
     to_own(0)
     gm.r4b()
     gm.r4c()
+    gq.drain()
+    go.drain()
     sib_copy(0).wait_recv()
     z_copy(0, 1).wait_recv()
+    z_copy(1, 0).wait_recv()
+    for k in range(4):
+        begin_rows(k)
+    z_copy(0, 0).wait_recv()
     z_copy(1, 1).wait_recv()
-    z_copy(0, 0).wait_recv()
-    z_copy(1, 0).wait_recv()
     for k in range(4):
         finish_rows(k)
 
@@ -604,6 +624,7 @@
     for step in range(1, 8):
         stat_copy(step).start()
     gm.finish()
+    gm.drain()
     for step in range(1, 8):
         stat_copy(step).wait_recv()
     means = [stats[i][0:1, :] for i in range(8)]
@@ -725,10 +746,10 @@
 
     for step in range(1, 8):
         deal_copy(step).wait_send()
-    for g in (gq, go, gm):
-        g.drain()
-    for dz in range(4):
+    for dz in (0, 1, 3):
         sib_copy(dz).wait_send()
+    for part in (0, 1):
+        sib_half(part).wait_send()
     for which in (0, 1):
         opp_copy(which).wait_send()
         for part in (0, 1):
@@ -814,8 +835,8 @@
             dma((10,)),
             dma((8,)),
             dma((8,)),
-            dma((4,)),
-            dma((4,)),
+            dma((5,)),
+            dma((5,)),
             dma((2,)),
             dma((2,)),
             dma((2, 2)),

time: 172 us -> 171 us (level)
  no operation moved by 1% of the time
where the time goes in v1:
time: 171 us
  Pallas kernels  166 us (97%)
  local copies, waits for them, and re-layouts  4.47 us (3%)
    pallas_call x1, Pallas kernels, per_device(): pl.pallas_call(kernel, out_shape=jax.ShapeDtypeStruct((16, 32, 256), BF16...  166 us

profile of v1, /device:TPU:0, one launch (start us, length us, event | category | flops | bytes accessed | tf_op | source)
XLA Modules:
  0.0 170.7 jit_solution(12629902340119284047)
XLA Ops:
  0.0 0.0 copy-start
  0.0 0.7 copy-done
  0.7 0.6 dynamic-slice_bitcast_fusion.own_ref
  1.3 0.9 dynamic-slice_reduce_fusion
  2.2 0.7 reshape.13.grid_ref
  2.8 166.2 %shard_map.109 = bf16[16,32,256]{2,1,0:T(8,128)(2,1)} custom-call(bf16[1024,4096]{1,0:T(8,128)(2,1)} %tokens.1, bf16[3,256,512]{2,1,0:T(8,128)(2,1)} %bitcast.8, bf16[512,256]{1,0:T(8,128)(2,1)} %wo.1, bf16[2,2,256,256]{3,2,1,0:T(8,128)(2,1)} %bitcast.9, f32[1,4096]{1,0:T(1,128)} %bitcast.10, f32[1,4096]{1,0:T(1,128)} %bitcast.11, f32[1,4096]{1,0:T(1,128)} %bitcast.12, ...), custom_call_target="tpu_custom_call" | custom-call | tf_op jit(solution)/shard_map/pallas_call | solution.py:792
  169.0 1.6 slice.3
Async XLA Ops:
  0.0 0.7 copy-start
